TPU v7x, 512 devices: a whole 4x8x8 slice. The times are simulated.
512 devices in a mesh: tm: 512 (over y, x, z, core).
Axes of the slice: x: 4, y: 8, z: 8, core: 2. Of those that a mesh axis runs over, the one named last changes fastest.
Arguments:
- inputs: float32 [256, 131072], P(None, 'tm'), may hold values from -6 to 6
- cotangent: float32 [256, 131072], P(None, 'tm'), may hold values from -6 to 6
- taps_far: float32 [3, 256, 256], replicated, may hold values from -0.21875 to 0.21875
- taps_near: float32 [3, 256, 256], replicated, may hold values from -0.21875 to 0.21875
- joining: float32 [256, 512], replicated, may hold values from -0.25 to 0.25
Outputs:
- input_grad: float32 [256, 131072], P(None, 'tm')
- far_grad: float32 [3, 256, 256], replicated
- near_grad: float32 [3, 256, 256], replicated
- joining_grad: float32 [256, 512], replicated
All inputs are finite; a program needn't handle non-finite values.
Results may differ from a plain program's by a relative error of at most 0.000071.
Values sent between devices are 32-bit elements; how exact they have to be, the bound alone decides.
A program may use at most 64 MiB of HBM per device.

v0:
```python
import math

import jax
import jax.numpy as jnp
from jax import lax
from jax.sharding import PartitionSpec as P

NEAR = 4


def passed_along(value, axis, steps):
    count = lax.axis_size(axis)
    initial, last = (max(0, -steps), min(count, count - steps))
    return lax.ppermute(value, axis, [(source, source + steps) for source in range(initial, last)])


def padded_2(x, sides, width):
    for axis, dim in sides:
        size, length = (lax.axis_size(axis), x.shape[dim])
        up = [(i, (i + 1) % size) for i in range(size - 1)]
        down = [(j, i) for i, j in up]
        last = lax.slice_in_dim(x, length - width, length, axis=dim)
        initial = lax.slice_in_dim(x, 0, width, axis=dim)
        before = lax.ppermute(last, axis, up)
        after = lax.ppermute(initial, axis, down)
        x = jnp.concatenate([before, x, after], axis=dim)
    return x


def product(left, right):
    return jnp.dot(left, right, precision=lax.Precision.HIGHEST, preferred_element_type=jnp.float32)


def outer_time(left, right):
    return lax.dot_general(
        left,
        right,
        (((1,), (1,)), ((), ())),
        precision=lax.Precision.HIGHEST,
        preferred_element_type=jnp.float32,
    )


def inner_rows(left, right):
    return lax.dot_general(
        left,
        right,
        (((0,), (0,)), ((), ())),
        precision=lax.Precision.HIGHEST,
        preferred_element_type=jnp.float32,
    )


def gelu_slope(value):
    inner = 0.7978845608 * (value + 0.044715 * value * value * value)
    hyper = jnp.tanh(inner)
    return 0.5 * (1.0 + hyper) + 0.5 * value * (1.0 - hyper * hyper) * 0.7978845608 * (
        1.0 + 3.0 * 0.044715 * value * value
    )


def on_device(inputs, cotangent, taps_far, taps_near, joining):
    width = inputs.shape[0]
    cols = inputs.shape[1]
    hops = lax.axis_size("tm") // 8
    scale = 1.0 / math.sqrt(cols * lax.axis_size("tm"))
    far_prev = passed_along(inputs, "tm", hops)
    far_next = passed_along(inputs, "tm", -hops)
    padded = padded_2(inputs, (("tm", 1),), NEAR)
    near_prev = padded[:, :cols]
    near_next = padded[:, 2 * NEAR : 2 * NEAR + cols]
    branch_far = (
        product(taps_far[0], far_prev)
        + product(taps_far[1], inputs)
        + product(taps_far[2], far_next)
    )
    branch_near = (
        product(taps_near[0], near_prev)
        + product(taps_near[1], inputs)
        + product(taps_near[2], near_next)
    )
    zvalue = product(joining[:, :width], branch_far) + product(joining[:, width:], branch_near)
    dzvalue = cotangent * gelu_slope(zvalue)
    joining_grad = jnp.concatenate(
        [outer_time(dzvalue, branch_far), outer_time(dzvalue, branch_near)], axis=1
    )
    d_far = inner_rows(joining[:, :width], dzvalue)
    d_near = inner_rows(joining[:, width:], dzvalue)
    dfar_next = passed_along(d_far, "tm", -hops)
    dfar_prev = passed_along(d_far, "tm", hops)
    dpadded = padded_2(d_near, (("tm", 1),), NEAR)
    dnear_prev = dpadded[:, :cols]
    dnear_next = dpadded[:, 2 * NEAR : 2 * NEAR + cols]
    input_grad = (
        cotangent
        + inner_rows(taps_far[0], dfar_next)
        + inner_rows(taps_far[1], d_far)
        + inner_rows(taps_far[2], dfar_prev)
    )
    input_grad = (
        input_grad
        + inner_rows(taps_near[0], dnear_next)
        + inner_rows(taps_near[1], d_near)
        + inner_rows(taps_near[2], dnear_prev)
    )
    again_prev = passed_along(inputs, "tm", hops)
    again_next = passed_along(inputs, "tm", -hops)
    again_padded = padded_2(inputs, (("tm", 1),), NEAR)
    far_grad = jnp.stack(
        [outer_time(d_far, again_prev), outer_time(d_far, inputs), outer_time(d_far, again_next)]
    )
    near_grad = jnp.stack(
        [
            outer_time(d_near, again_padded[:, :cols]),
            outer_time(d_near, inputs),
            outer_time(d_near, again_padded[:, 2 * NEAR : 2 * NEAR + cols]),
        ]
    )
    far_grad, near_grad, joining_grad = lax.psum((far_grad, near_grad, joining_grad), "tm")
    return (input_grad, far_grad * scale, near_grad * scale, joining_grad * scale)


def solution(mesh):
    in_specs = (P(None, "tm"), P(None, "tm"), P(), P(), P())
    out_specs = (P(None, "tm"), P(), P(), P())
    return jax.shard_map(
        on_device, mesh=mesh, in_specs=in_specs, out_specs=out_specs, check_vma=False
    )
```

profile of v0, /device:TPU:1, one launch (start us, length us, event | category | flops | bytes accessed | tf_op | source)
XLA Modules:
  0.0 341.0 jit_solution(7144143807142882396)
XLA Ops:
  7.2 1.4 collective-permute-start.1
  8.7 4.7 %collective-permute-start = (f32[256,256]{1,0:T(8,128)}, f32[256,256]{1,0:T(8,128)S(1)}, u32[]{:S(2)}, u32[]{:S(2)}) collective-permute-start(f32[256,256]{1,0:T(8,128)} %param.5), channel_id=1, source_target_pairs={{0,64},{1,65},{2,66},{3,67},{4,68},{5,69},{6,70},{7,71},{8,72},{9,... | collective-permute-start | bytes 786440 | tf_op jit(solution)/shard_map/ppermute | solution.py:14
  13.3 1.1 fusion.59
  14.4 5.3 %collective-permute-start.2 = (f32[256,4]{1,0:T(8,128)S(1)}, f32[256,4]{1,0:T(8,128)S(1)}, u32[]{:S(2)}, u32[]{:S(2)}) collective-permute-start(f32[256,4]{1,0:T(8,128)S(1)} %get-tuple-element.14), channel_id=1, source_target_pairs={{0,1},{1,2},{2,3},{3,4},{4,5},{5,6},{6,7},{7,8},{8,9},{9,10},{10,1... | collective-permute-start | bytes 12296 | tf_op jit(solution)/shard_map/ppermute | solution.py:24
  19.7 4.7 %collective-permute-start.3 = (f32[256,4]{1,0:T(8,128)S(1)}, f32[256,4]{1,0:T(8,128)S(1)}, u32[]{:S(2)}, u32[]{:S(2)}) collective-permute-start(f32[256,4]{1,0:T(8,128)S(1)} %get-tuple-element.13), channel_id=1, source_target_pairs={{1,0},{2,1},{3,2},{4,3},{5,4},{6,5},{7,6},{8,7},{9,8},{10,9},{11,1... | collective-permute-start | bytes 12296 | tf_op jit(solution)/shard_map/ppermute | solution.py:25
  24.4 1.3 fusion.29
  25.8 0.6 fusion.21
  26.9 0.7 fusion.7
  27.6 0.7 fusion.6
  29.6 0.6 copy-done.3
  30.2 0.6 fusion.44
  32.5 0.6 convolution_bitcast_fusion.1
  33.1 0.6 fusion.61
  34.1 1.9 collective-permute-start.6
  36.0 0.6 convolution_bitcast_fusion.4
  36.6 1.3 collective-permute-start.4
  37.9 0.8 pad_maximum_fusion.2
  38.8 0.6 convolution_bitcast_fusion.3
  39.4 0.6 convolution_bitcast_fusion.5
  40.0 0.9 pad_maximum_fusion
  40.9 0.7 convolution_bitcast_fusion
  41.6 0.7 convolution_bitcast_fusion.2
  42.3 0.9 pad_maximum_fusion.1
  43.7 10.1 %collective-permute-start.5 = (f32[256,256]{0,1:T(8,128)S(1)}, f32[256,256]{0,1:T(8,128)S(1)}, u32[]{:S(2)}, u32[]{:S(2)}) collective-permute-start(f32[256,256]{0,1:T(8,128)S(1)} %bitcast.110), channel_id=1, source_target_pairs={{0,64},{1,65},{2,66},{3,67},{4,68},{5,69},{6,70},{7,71},{8,72},{9,... | collective-permute-start | bytes 786440 | tf_op jit(solution)/shard_map/ppermute | solution.py:14
  53.8 1.9 collective-permute-start.7
  56.1 1.3 fusion.4
  57.9 2.1 collective-permute-done.7
  60.4 0.8 copy.12
  61.2 269.3 %all-reduce.3.cloned.1.call-done = (f32[3,256,256]{2,1,0:T(8,128)}, f32[3,256,256]{2,1,0:T(8,128)}, f32[256,512]{0,1:T(8,128)}) async-done(((f32[3,256,256]{2,1,0:T(8,128)}, f32[3,256,256]{2,1,0:T(8,128)}, f32[256,512]{0,1:T(8,128)}), (f32[3,256,256]{2,1,0:T(8,128)}, f32[3,256,256]{2,1,0:T(8,128)}, f32[256,512]{0,1:T(8,128)})) %all-reduce.3.cloned.1.call-update) | async-done | bytes 2097168 | tf_op jit(solution)/shard_map/psum | solution.py:119
  330.6 1.2 broadcast_multiply_fusion.2
  331.7 1.0 copy.13
  332.9 1.3 broadcast_multiply_fusion
  (39 shorter events, 5.6 us)
Async XLA Ops:
  7.2 17.2 %copy-start = (f32[256,256]{1,0:T(8,128)S(1)}, f32[256,256]{1,0:T(8,128)}, u32[]{:S(2)}) copy-start(f32[256,256]{1,0:T(8,128)} %param.5) | copy-start | bytes 786436
  7.2 18.6 %copy-start.2 = (f32[3,256,256]{2,1,0:T(8,128)S(1)}, f32[3,256,256]{2,1,0:T(8,128)}, u32[]{:S(2)}) copy-start(f32[3,256,256]{2,1,0:T(8,128)} %param.8) | copy-start | bytes 2359300
  7.2 323.4 %all-reduce.3.cloned.1.call-start = ((), (), s32[]{:S(2)}) async-start(), calls=%async_computation | async-start | bytes 4194304 | tf_op jit(solution)/shard_map/psum | solution.py:119
  7.2 21.1 %collective-permute-start.1 = (f32[256,256]{1,0:T(8,128)}, f32[256,256]{1,0:T(8,128)S(1)}, u32[]{:S(2)}, u32[]{:S(2)}) collective-permute-start(f32[256,256]{1,0:T(8,128)} %param.5), channel_id=1, source_target_pairs={{64,0},{65,1},{66,2},{67,3},{68,4},{69,5},{70,6},{71,7},{72,8},{73... | collective-permute-start | bytes 786440 | tf_op jit(solution)/shard_map/ppermute | solution.py:14
  8.7 20.5 %collective-permute-start = (f32[256,256]{1,0:T(8,128)}, f32[256,256]{1,0:T(8,128)S(1)}, u32[]{:S(2)}, u32[]{:S(2)}) collective-permute-start(f32[256,256]{1,0:T(8,128)} %param.5), channel_id=1, source_target_pairs={{0,64},{1,65},{2,66},{3,67},{4,68},{5,69},{6,70},{7,71},{8,72},{9,... | collective-permute-start | bytes 786440 | tf_op jit(solution)/shard_map/ppermute | solution.py:14
  14.4 12.4 %collective-permute-start.2 = (f32[256,4]{1,0:T(8,128)S(1)}, f32[256,4]{1,0:T(8,128)S(1)}, u32[]{:S(2)}, u32[]{:S(2)}) collective-permute-start(f32[256,4]{1,0:T(8,128)S(1)} %get-tuple-element.14), channel_id=1, source_target_pairs={{0,1},{1,2},{2,3},{3,4},{4,5},{5,6},{6,7},{7,8},{8,9},{9,10},{10,1... | collective-permute-start | bytes 12296 | tf_op jit(solution)/shard_map/ppermute | solution.py:24
  19.7 7.9 %collective-permute-start.3 = (f32[256,4]{1,0:T(8,128)S(1)}, f32[256,4]{1,0:T(8,128)S(1)}, u32[]{:S(2)}, u32[]{:S(2)}) collective-permute-start(f32[256,4]{1,0:T(8,128)S(1)} %get-tuple-element.13), channel_id=1, source_target_pairs={{1,0},{2,1},{3,2},{4,3},{5,4},{6,5},{7,6},{8,7},{9,8},{10,9},{11,1... | collective-permute-start | bytes 12296 | tf_op jit(solution)/shard_map/ppermute | solution.py:25
  25.8 1.0 copy-start.8
  27.6 1.2 copy-start.1
  27.6 0.8 copy-start.6
  29.1 1.0 copy-start.3
  34.1 21.6 %collective-permute-start.6 = (f32[256,4]{0,1:T(4,128)S(1)}, f32[256,4]{0,1:T(4,128)S(1)}, u32[]{:S(2)}, u32[]{:S(2)}) collective-permute-start(f32[256,4]{0,1:T(4,128)S(1)} %get-tuple-element.12), channel_id=1, source_target_pairs={{1,0},{2,1},{3,2},{4,3},{5,4},{6,5},{7,6},{8,7},{9,8},{10,9},{11,1... | collective-permute-start | bytes 12296 | tf_op jit(solution)/shard_map/ppermute | solution.py:25
  36.6 19.5 %collective-permute-start.4 = (f32[256,256]{0,1:T(8,128)S(1)}, f32[256,256]{0,1:T(8,128)}, u32[]{:S(2)}, u32[]{:S(2)}) collective-permute-start(f32[256,256]{0,1:T(8,128)S(1)} %bitcast.109), channel_id=1, source_target_pairs={{64,0},{65,1},{66,2},{67,3},{68,4},{69,5},{70,6},{71,7},{72,8},{73... | collective-permute-start | bytes 786440 | tf_op jit(solution)/shard_map/ppermute | solution.py:14
  40.0 0.9 copy-start.7
  43.7 13.8 %collective-permute-start.5 = (f32[256,256]{0,1:T(8,128)S(1)}, f32[256,256]{0,1:T(8,128)S(1)}, u32[]{:S(2)}, u32[]{:S(2)}) collective-permute-start(f32[256,256]{0,1:T(8,128)S(1)} %bitcast.110), channel_id=1, source_target_pairs={{0,64},{1,65},{2,66},{3,67},{4,68},{5,69},{6,70},{7,71},{8,72},{9,... | collective-permute-start | bytes 786440 | tf_op jit(solution)/shard_map/ppermute | solution.py:14
  53.8 6.2 %collective-permute-start.7 = (f32[256,4]{0,1:T(4,128)S(1)}, f32[256,4]{0,1:T(4,128)S(1)}, u32[]{:S(2)}, u32[]{:S(2)}) collective-permute-start(f32[256,4]{0,1:T(4,128)S(1)} %get-tuple-element.11), channel_id=1, source_target_pairs={{0,1},{1,2},{2,3},{3,4},{4,5},{5,6},{6,7},{7,8},{8,9},{9,10},{10,1... | collective-permute-start | bytes 12296 | tf_op jit(solution)/shard_map/ppermute | solution.py:24
  330.6 2.2 copy-start.5
  331.7 1.2 copy-start.4
Sparse Core Ops, SparseCore 0:
  43.4 287.1 all-reduce.2
where the time goes:
time: 342 us; the launch traced here: 341 us
  waiting for transfers between devices  271 us (79%)
  starting transfers between devices  31.3 us (9%)
  between operations  14.5 us (4%)
  matrix products  14 us (4%)
  other arithmetic  5.13 us (2%)
  local copies, waits for them, and re-layouts  4.59 us (1%)
    psum x1, waiting for transfers between devices, on_device(): lax.psum((far_grad, near_grad, joining_grad), 'tm')  269 us
    ppermute x4, starting transfers between devices, passed_along(): lax.ppermute(value, axis, [(source, source + steps) for source in range(i...  17.5 us
    ppermute x2, starting transfers between devices, padded_2(): before = lax.ppermute(last, axis, up)  7.2 us
  transfers between devices with their start and end apart: 9, of which 2 were waited for; matrix products, arithmetic and copies ran while one was open for 4% of the time, Pallas kernels for 0%

commit v1 on v0

v1 whole, which is shorter than its diff:
```python
import functools
import math

import jax
import jax.numpy as jnp
from jax import lax
from jax.experimental import pallas as pl
from jax.experimental.pallas import tpu as pltpu
from jax.sharding import PartitionSpec as P

NEAR = 4
C = 256
L = 128
Y, X, Z = 8, 4, 8
MESH = pl.DeviceIdType.MESH
F32 = jnp.float32
BF16 = jnp.bfloat16
NA = 96 // (X * Z)
NB = 64 // (X * Z)
GA, GB = NA * Z, NB * X
NN = (((1,), (0,)), ((), ()))
NT = (((1,), (1,)), ((), ()))


def split(v):
    hi = v.astype(BF16)
    return hi, (v - hi.astype(F32)).astype(BF16)


def mm3(a, b, dims):
    dot = functools.partial(lax.dot_general, dimension_numbers=dims, preferred_element_type=F32)
    return dot(a[0], b[0]) + (dot(a[0], b[1]) + dot(a[1], b[0]))


def gelu_slope(value):
    inner = 0.7978845608 * (value + 0.044715 * value * value * value)
    hyper = jnp.tanh(inner)
    return 0.5 * (1.0 + hyper) + 0.5 * value * (1.0 - hyper * hyper) * 0.7978845608 * (
        1.0 + 3.0 * 0.044715 * value * value
    )


def shifted(b0, b1, p, n):
    lane = lax.broadcasted_iota(jnp.int32, (C, L), 1)
    low, high = lane < NEAR, lane >= L - NEAR
    r0, r1, rp = (pltpu.roll(v, NEAR, 1) for v in (b0, b1, p))
    s0, s1, sn = (pltpu.roll(v, L - NEAR, 1) for v in (b0, b1, n))
    back = jnp.concatenate([jnp.where(low, rp, r0), jnp.where(low, r0, r1)], axis=1)
    ahead = jnp.concatenate([jnp.where(high, s1, s0), jnp.where(high, sn, s1)], axis=1)
    return back, ahead


def kernel(
    scale,
    x_in, cot_in, tf_in, tn_in, j_in,
    ig_out, far_out, near_out, join_out,
    xv, cotv, tfv, tnv, jv,
    xfar, xnear, dfar, dnear, dz,
    xh, xl, ah, al, th, tl, ath, atl, jth, jtl, dh, dl, zacc, igv,
    s0, s1, rc, ra1, rb1, s2a, s2b, ra2, rb2, ry, full,
    farv, nearv, joinv,
    lsem, osem, xs, xr, ds, dr, cs, cr,
    as1, ar1, bs1, br1, as2, ar2, bs2, br2, ys, yr,
    gas1, gar1, gbs1, gbr1, gas2, gar2, gbs2, gbr2, fas, far_, fbs, fbr,
):
    me = lax.axis_index("tm")
    c = lax.rem(me, 2)
    z = lax.rem(me // 2, Z)
    x = lax.rem(me // (2 * Z), X)
    y = me // (2 * Z * X)
    total = 2 * X * Y * Z

    def at(yy, xx, zz, cc):
        return ((yy * X + xx) * Z + zz) * 2 + cc

    def ypeer(d):
        return at(lax.rem(y + d, Y), x, z, c)

    def xpeer(d):
        return at(y, lax.rem(x + d, X), z, c)

    def zpeer(d):
        return at(y, x, lax.rem(z + d, Z), c)

    sibling = at(y, x, z, 1 - c)
    later, earlier = lax.rem(me + 1, total), lax.rem(me + total - 1, total)
    ys_, xs_, zs_ = range(1, Y), range(1, X), range(1, Z)
    zorder = [4, 3, 5, 2, 6, 1, 7]
    yorder = [4, 3, 5, 2, 6, 1, 7]
    xorder = [2, 1, 3]
    started = []

    def send(src, dst, ssem, rsem, device):
        copy = pltpu.make_async_remote_copy(
            src_ref=src, dst_ref=dst, send_sem=ssem, recv_sem=rsem, device_id=(device,), device_id_type=MESH
        )
        copy.start()
        started.append(copy)
        return copy

    def local(src, dst, sem):
        copy = pltpu.make_async_copy(src, dst, sem)
        copy.start()
        return copy

    partners = [ypeer(d) for d in ys_] + [xpeer(d) for d in xs_] + [zpeer(d) for d in zs_] + [later, earlier]
    barrier = pltpu.get_barrier_semaphore()
    for partner in partners + [at(y, x, z, 1 - c)]:
        pl.semaphore_signal(barrier, inc=1, device_id=(partner,), device_id_type=MESH)
    loads = [
        local(src, dst, lsem.at[k])
        for k, (src, dst) in enumerate(
            [(j_in, jv), (tf_in, tfv), (tn_in, tnv), (x_in, xv), (cot_in, cotv)]
        )
    ]
    pl.semaphore_wait(barrier, len(partners) + 1)

    up, down = ypeer(1), ypeer(Y - 1)
    xf = [
        send(x_in, xfar.at[0], xs.at[0], xr.at[0], up),
        send(x_in, xfar.at[1], xs.at[1], xr.at[1], down),
    ]
    xn = [
        send(x_in.at[:, pl.ds(L, L)], xnear.at[0], xs.at[2], xr.at[2], later),
        send(x_in.at[:, pl.ds(0, L)], xnear.at[1], xs.at[3], xr.at[3], earlier),
    ]
    one = lambda ok: jnp.where(ok, 1.0, 0.0).astype(F32)
    has_up, has_down = one(y < Y - 1), one(y > 0)
    has_later, has_earlier = one(me < total - 1), one(me > 0)

    def put(hi, lo, k, v):
        hi[k], lo[k] = split(v)

    def get(hi, lo, k):
        return hi[k], lo[k]

    for copy in loads[:3]:
        copy.wait()
    jf, jn = split(jv[:, :C]), split(jv[:, C:])
    for k in range(3):
        put(th, tl, k, tfv[k])
        put(th, tl, 3 + k, tnv[k])
    joined = [
        mm3(jf, get(th, tl, 0), NN),
        mm3(jf, get(th, tl, 1), NN) + mm3(jn, get(th, tl, 4), NN),
        mm3(jf, get(th, tl, 2), NN),
        mm3(jn, get(th, tl, 3), NN),
        mm3(jn, get(th, tl, 5), NN),
    ]
    for k, v in enumerate(joined):
        put(ah, al, k, v)
    for copy in loads[3:]:
        copy.wait()
    put(xh, xl, 1, xv[...])
    xn[0].wait_recv()
    xn[1].wait_recv()
    back, ahead = shifted(xv[:, :L], xv[:, L:], xnear[0] * has_earlier, xnear[1] * has_later)
    put(xh, xl, 3, back)
    put(xh, xl, 4, ahead)
    zacc[...] = sum(mm3(get(ah, al, k), get(xh, xl, k), NN) for k in (1, 3, 4))
    for k, v in enumerate(joined):
        put(ath, atl, k, v.T)
    put(jth, jtl, 0, jv[:, :C].T)
    put(jth, jtl, 1, jv[:, C:].T)

    xf[0].wait_recv()
    put(xh, xl, 0, xfar[0] * has_down)
    xf[1].wait_recv()
    put(xh, xl, 2, xfar[1] * has_up)
    zvalue = zacc[...] + (mm3(get(ah, al, 0), get(xh, xl, 0), NN) + mm3(get(ah, al, 2), get(xh, xl, 2), NN))
    dzvalue = cotv[...] * gelu_slope(zvalue)
    dz[...] = dzvalue
    dh[...], dl[...] = split(dzvalue)
    df = [
        send(dz, dfar.at[0], ds.at[0], dr.at[0], up),
        send(dz, dfar.at[1], ds.at[1], dr.at[1], down),
    ]

    for half, out in ((1 - c, s1), (c, s0)):
        rows = pl.ds(pl.multiple_of(half * L, L), L)
        part = dh[rows, :], dl[rows, :]
        for k in range(5):
            g = mm3(part, get(xh, xl, k), NT)
            out[pl.ds(32 * k, 16)] = g[:, :L].reshape(16, 8, L)
            out[pl.ds(32 * k + 16, 16)] = g[:, L:].reshape(16, 8, L)
        if out is s1:
            core = [send(s1, rc, cs.at[0], cr.at[0], sibling)]
    dn = [
        send(dz.at[:, pl.ds(L, L)], dnear.at[0], ds.at[2], dr.at[2], later),
        send(dz.at[:, pl.ds(0, L)], dnear.at[1], ds.at[3], dr.at[3], earlier),
    ]
    core[0].wait_recv()
    s0[...] = s0[...] + rc[...]

    p1a = [
        send(s0.at[pl.ds(GA * lax.rem(x + d, X), GA)], ra1.at[d - 1], as1.at[d - 1], ar1.at[d - 1], xpeer(d))
        for d in xorder
    ]
    p1b = [
        send(s0.at[pl.ds(96 + GB * lax.rem(z + d, Z), GB)], rb1.at[d - 1], bs1.at[d - 1], br1.at[d - 1], zpeer(d))
        for d in zorder
    ]
    igv[...] = cotv[...] + mm3(get(ath, atl, 1), (dh[...], dl[...]), NN)
    for copy in p1a:
        copy.wait_recv()
    s2a[...] = s0[pl.ds(GA * x, GA)] + sum(ra1[d - 1] for d in xs_)
    p2a = [
        send(s2a.at[pl.ds(NA * lax.rem(z + d, Z), NA)], ra2.at[d - 1], as2.at[d - 1], ar2.at[d - 1], zpeer(d))
        for d in zorder
    ]
    for copy in p1b:
        copy.wait_recv()
    s2b[...] = s0[pl.ds(96 + GB * z, GB)] + sum(rb1[d - 1] for d in zs_)
    p2b = [
        send(s2b.at[pl.ds(NB * lax.rem(x + d, X), NB)], rb2.at[d - 1], bs2.at[d - 1], br2.at[d - 1], xpeer(d))
        for d in xorder
    ]

    dn[0].wait_recv()
    dn[1].wait_recv()
    back, ahead = shifted(dz[:, :L], dz[:, L:], dnear[0] * has_earlier, dnear[1] * has_later)
    acc = mm3(get(ath, atl, 3), split(ahead), NN) + mm3(get(ath, atl, 4), split(back), NN)
    df[0].wait_recv()
    df[1].wait_recv()
    acc += mm3(get(ath, atl, 0), split(dfar[1] * has_up), NN) + mm3(get(ath, atl, 2), split(dfar[0] * has_down), NN)
    igv[...] = igv[...] + acc
    outs = [local(igv, ig_out, osem.at[0])]

    for copy in p2a + p2b:
        copy.wait_recv()
    mine = ry.at[y]
    mine[pl.ds(0, NA)] = s2a[pl.ds(NA * z, NA)] + sum(ra2[d - 1] for d in zs_)
    mine[pl.ds(NA, NB)] = s2b[pl.ds(NB * x, NB)] + sum(rb2[d - 1] for d in xs_)
    p3 = [send(mine, ry.at[y], ys.at[d - 1], yr.at[d - 1], ypeer(d)) for d in yorder]
    for copy in p3:
        copy.wait_recv()
    summed = ry[0]
    for k in range(1, Y):
        summed = summed + ry[k]
    fa = full.at[c, pl.ds(GA * x + NA * z, NA)]
    fb = full.at[c, pl.ds(96 + GB * z + NB * x, NB)]
    fa[...] = summed[:NA]
    fb[...] = summed[NA:]

    g1a = [send(fa, fa, gas1.at[d - 1], gar1.at[d - 1], zpeer(d)) for d in zorder]
    g1b = [send(fb, fb, gbs1.at[d - 1], gbr1.at[d - 1], xpeer(d)) for d in xorder]

    def block_a(xx):
        return full.at[c, pl.ds(GA * xx, GA)]

    def block_b(zz):
        return full.at[c, pl.ds(96 + GB * zz, GB)]

    for copy in g1a:
        copy.wait_recv()
    g2a = {d: send(block_a(x), block_a(x), gas2.at[d - 1], gar2.at[d - 1], xpeer(d)) for d in xorder}
    for copy in g1b:
        copy.wait_recv()
    g2b = {d: send(block_b(z), block_b(z), gbs2.at[d - 1], gbr2.at[d - 1], zpeer(d)) for d in zorder}
    forward_a = [send(block_a(x), block_a(x), fas.at[0], far_.at[0], sibling)]
    forward_b = [send(block_b(z), block_b(z), fbs.at[0], fbr.at[0], sibling)]
    for d in (1, 3, 2):
        g2a[d].wait_recv()
        block = block_a(lax.rem(x - d + X, X))
        forward_a.append(send(block, block, fas.at[d], far_.at[d], sibling))
    for d in (1, 7, 2, 6, 3, 5, 4):
        g2b[d].wait_recv()
        block = block_b(lax.rem(z - d + Z, Z))
        forward_b.append(send(block, block, fbs.at[d], fbr.at[d], sibling))
    for copy in forward_a:
        copy.wait_recv()

    def gathered(k):
        rows = [
            jnp.concatenate([full[h, pl.ds(32 * k + 16 * q, 16)].reshape(L, L) for q in (0, 1)], axis=1)
            for h in (0, 1)
        ]
        return split(jnp.concatenate(rows, axis=0))

    def grads(js, terms, out, jout, col):
        jacc = None
        for k, tap, slot in terms:
            g = gathered(k)
            out[slot] = mm3(get(jth, jtl, js), g, NN) * scale
            term = mm3(g, get(th, tl, tap), NT)
            jacc = term if jacc is None else jacc + term
        jout[:, col : col + C] = jacc * scale

    grads(0, [(0, 0, 0), (1, 1, 1), (2, 2, 2)], farv, joinv, 0)
    outs.append(local(farv, far_out, osem.at[1]))
    for copy in forward_b:
        copy.wait_recv()
    grads(1, [(3, 3, 0), (1, 4, 1), (4, 5, 2)], nearv, joinv, C)
    outs.append(local(nearv, near_out, osem.at[2]))
    outs.append(local(joinv, join_out, osem.at[3]))
    for copy in started:
        copy.wait_send()
    for copy in outs:
        copy.wait()


def on_device(inputs, cotangent, taps_far, taps_near, joining):
    scale = 1.0 / math.sqrt(inputs.shape[1] * lax.axis_size("tm"))
    sq = (C, C)
    vm = lambda *shape: pltpu.VMEM(shape, F32)
    vb = lambda *shape: pltpu.VMEM(shape, BF16)
    dma = lambda n: pltpu.SemaphoreType.DMA((n,))
    anywhere = pl.BlockSpec(memory_space=pl.ANY)
    scratch = (
        [vm(*sq), vm(*sq), vm(3, *sq), vm(3, *sq), vm(C, 2 * C)]
        + [vm(2, *sq), vm(2, C, L), vm(2, *sq), vm(2, C, L), vm(*sq)]
        + [vb(5, *sq)] * 4 + [vb(6, *sq)] * 2 + [vb(5, *sq)] * 2 + [vb(2, *sq)] * 2 + [vb(*sq)] * 2
        + [vm(*sq), vm(*sq)]
        + [vm(160, 8, L)] * 3
        + [vm(X - 1, GA, 8, L), vm(Z - 1, GB, 8, L), vm(GA, 8, L), vm(GB, 8, L)]
        + [vm(Z - 1, NA, 8, L), vm(X - 1, NB, 8, L), vm(Y, NA + NB, 8, L), vm(2, 160, 8, L)]
        + [vm(3, *sq), vm(3, *sq), vm(C, 2 * C)]
        + [dma(5), dma(4), dma(4), dma(4), dma(4), dma(4), dma(1), dma(1)]
        + [dma(X - 1)] * 2 + [dma(Z - 1)] * 2 + [dma(Z - 1)] * 2 + [dma(X - 1)] * 2 + [dma(Y - 1)] * 2
        + [dma(Z - 1)] * 2 + [dma(X - 1)] * 2 + [dma(X - 1)] * 2 + [dma(Z - 1)] * 2
        + [dma(X)] * 2 + [dma(Z)] * 2
    )
    return pl.pallas_call(
        functools.partial(kernel, scale),
        out_shape=[
            jax.ShapeDtypeStruct(sq, F32),
            jax.ShapeDtypeStruct((3, *sq), F32),
            jax.ShapeDtypeStruct((3, *sq), F32),
            jax.ShapeDtypeStruct((C, 2 * C), F32),
        ],
        in_specs=[anywhere] * 5,
        out_specs=[anywhere] * 4,
        scratch_shapes=scratch,
        compiler_params=pltpu.CompilerParams(
            collective_id=0, has_side_effects=True, vmem_limit_bytes=48 * 1024 * 1024
        ),
    )(inputs, cotangent, taps_far, taps_near, joining)


def solution(mesh):
    in_specs = (P(None, "tm"), P(None, "tm"), P(), P(), P())
    out_specs = (P(None, "tm"), P(), P(), P())
    return jax.shard_map(
        on_device, mesh=mesh, in_specs=in_specs, out_specs=out_specs, check_vma=False
    )
```

time: 342 us -> 71 us (0.21)
  waiting for transfers between devices: 271 us -> 0 us
  Pallas kernels: 0 us -> 61.5 us
  starting transfers between devices: 31.3 us -> 0 us
  matrix products: 14 us -> 0 us
  between operations: 14.5 us -> 0.65 us
  other arithmetic: 5.13 us -> 0 us
  local copies, waits for them, and re-layouts: 4.59 us -> 8.45 us
    psum x1 -> x0, waiting for transfers between devices: 269 us -> none  [on_device(): lax.psum((far_grad, near_grad, joining_grad), 'tm')]
    pallas_call x0 -> x1, Pallas kernels: none -> 61.5 us  [on_device(): pl.pallas_call(functools.partial(kernel, scale), out_shape=[jax.ShapeDtyp...]
    ppermute x8 -> x0, starting transfers between devices: 31.3 us -> none  [the longest x4 17.5 us: passed_along(): lax.ppermute(value, axis, [(source, source + steps) for source in range(i...]
    dot_general x24 -> x0, matrix products: 14 us -> none  [the longest x8 5.27 us: product(): jnp.dot(left, right, precision=lax.Precision.HIGHEST, preferred_element_t...]
    unnamed x21 -> x14, local copies, waits for them, and re-layouts: 3.53 us -> 8.45 us
  transfers between devices with their start and end apart: 9 -> 0, of which waited for: 2 -> 0; matrix products, arithmetic and copies ran while one was open for 4% -> 0% of each run, Pallas kernels for 0% -> 0%
where the time goes in v1:
time: 71 us; the launch traced here: 70.7 us
  Pallas kernels  61.5 us (87%)
  local copies, waits for them, and re-layouts  8.45 us (12%)
    pallas_call x1, Pallas kernels, on_device(): pl.pallas_call(functools.partial(kernel, scale), out_shape=[jax.ShapeDtyp...  61.5 us
    unnamed x14, local copies, waits for them, and re-layouts  8.45 us

profile of v1, /device:TPU:1, one launch (start us, length us, event | category | flops | bytes accessed | tf_op | source)
XLA Modules:
  0.0 70.7 jit_solution(3023703529061316133)
XLA Ops:
  0.6 0.0 copy-start
  0.6 1.1 %copy-done = f32[3,256,256]{2,1,0:T(8,128)S(1)} copy-done((f32[3,256,256]{2,1,0:T(8,128)S(1)}, f32[3,256,256]{2,1,0:T(8,128)}, u32[]{:S(2)}) %copy-start) | copy-done | bytes 786456
  1.8 0.0 copy-start.1
  1.8 1.1 %copy-done.1 = f32[3,256,256]{2,1,0:T(8,128)S(1)} copy-done((f32[3,256,256]{2,1,0:T(8,128)S(1)}, f32[3,256,256]{2,1,0:T(8,128)}, u32[]{:S(2)}) %copy-start.1) | copy-done | bytes 786456
  2.9 0.0 copy-start.2
  2.9 1.0 %copy-done.2 = f32[256,512]{1,0:T(8,128)S(1)} copy-done((f32[256,512]{1,0:T(8,128)S(1)}, f32[256,512]{1,0:T(8,128)}, u32[]{:S(2)}) %copy-start.2) | copy-done | bytes 524312
  3.9 0.0 copy-start.3
  3.9 0.9 %copy-done.3 = f32[256,256]{1,0:T(8,128)S(1)} copy-done((f32[256,256]{1,0:T(8,128)S(1)}, f32[256,256]{1,0:T(8,128)}, u32[]{:S(2)}) %copy-start.3) | copy-done | bytes 262168
  4.9 0.0 copy-start.4
  4.9 0.9 %copy-done.4 = f32[256,256]{1,0:T(8,128)S(1)} copy-done((f32[256,256]{1,0:T(8,128)S(1)}, f32[256,256]{1,0:T(8,128)}, u32[]{:S(2)}) %copy-start.4) | copy-done | bytes 262168
  5.8 61.5 %shard_map.84 = (f32[256,256]{1,0:T(8,128)S(1)}, f32[3,256,256]{2,1,0:T(8,128)S(1)}, f32[3,256,256]{2,1,0:T(8,128)S(1)}, f32[256,512]{1,0:T(8,128)S(1)}) custom-call(f32[256,256]{1,0:T(8,128)S(1)} %copy-done.3, f32[256,256]{1,0:T(8,128)S(1)} %copy-done.4, f32[3,256,256]{2,1,0:T(8,128)S(1)} %copy-done, f32[3,256,256]{2,1,0:T(8,128)S(1)} %copy-done.1, ...), custom_call_target="tpu_custom_call" | custom-call | tf_op jit(solution)/shard_map/pallas_call | solution.py:323
  67.4 0.7 copy.13
  68.1 0.9 %copy.14 = f32[3,256,256]{2,1,0:T(8,128)} copy(f32[3,256,256]{2,1,0:T(8,128)S(1)} %get-tuple-element.9) | data formatting | bytes 1572864
  69.0 0.9 %copy.15 = f32[3,256,256]{2,1,0:T(8,128)} copy(f32[3,256,256]{2,1,0:T(8,128)S(1)} %get-tuple-element.10) | data formatting | bytes 1572864
  69.9 0.8 %copy.16 = f32[256,512]{1,0:T(8,128)} copy(f32[256,512]{1,0:T(8,128)S(1)} %get-tuple-element.11) | data formatting | bytes 1048576
Async XLA Ops:
  0.6 1.1 %copy-start = (f32[3,256,256]{2,1,0:T(8,128)S(1)}, f32[3,256,256]{2,1,0:T(8,128)}, u32[]{:S(2)}) copy-start(f32[3,256,256]{2,1,0:T(8,128)} %tf_in.1) | copy-start | bytes 2359300
  1.8 1.1 %copy-start.1 = (f32[3,256,256]{2,1,0:T(8,128)S(1)}, f32[3,256,256]{2,1,0:T(8,128)}, u32[]{:S(2)}) copy-start(f32[3,256,256]{2,1,0:T(8,128)} %tn_in.1) | copy-start | bytes 2359300
  2.9 1.0 %copy-start.2 = (f32[256,512]{1,0:T(8,128)S(1)}, f32[256,512]{1,0:T(8,128)}, u32[]{:S(2)}) copy-start(f32[256,512]{1,0:T(8,128)} %j_in.1) | copy-start | bytes 1572868
  3.9 0.9 %copy-start.3 = (f32[256,256]{1,0:T(8,128)S(1)}, f32[256,256]{1,0:T(8,128)}, u32[]{:S(2)}) copy-start(f32[256,256]{1,0:T(8,128)} %x_in.1) | copy-start | bytes 786436
  4.9 0.9 %copy-start.4 = (f32[256,256]{1,0:T(8,128)S(1)}, f32[256,256]{1,0:T(8,128)}, u32[]{:S(2)}) copy-start(f32[256,256]{1,0:T(8,128)} %cot_in.1) | copy-start | bytes 786436

commit v2 on v1

v2 whole, which is shorter than its diff:
```python
import functools
import math

import jax
import jax.numpy as jnp
from jax import lax
from jax.experimental import pallas as pl
from jax.experimental.pallas import tpu as pltpu
from jax.sharding import PartitionSpec as P

NEAR = 4
C = 256
L = 128
Y, X, Z = 8, 4, 8
MESH = pl.DeviceIdType.MESH
F32 = jnp.float32
BF16 = jnp.bfloat16
M = 32
NA = 4 * M // (X * Z)
NB = M // (X * Z)
B0 = 4 * M
GA, GB = NA * Z, NB * X
NN = (((1,), (0,)), ((), ()))
NT = (((1,), (1,)), ((), ()))


def split(v):
    hi = v.astype(BF16)
    return hi, (v - hi.astype(F32)).astype(BF16)


def mm3(a, b, dims):
    dot = functools.partial(lax.dot_general, dimension_numbers=dims, preferred_element_type=F32)
    both = dot(jnp.concatenate(a, axis=0), b[0])
    return both[:C] + (both[C:] + dot(a[0], b[1]))


def gelu_slope(value):
    inner = 0.7978845608 * (value + 0.044715 * value * value * value)
    hyper = jnp.tanh(inner)
    return 0.5 * (1.0 + hyper) + 0.5 * value * (1.0 - hyper * hyper) * 0.7978845608 * (
        1.0 + 3.0 * 0.044715 * value * value
    )


def shifted(b0, b1, p, n):
    lane = lax.broadcasted_iota(jnp.int32, (C, L), 1)
    low, high = lane < NEAR, lane >= L - NEAR
    r0, r1, rp = (pltpu.roll(v, NEAR, 1) for v in (b0, b1, p))
    s0, s1, sn = (pltpu.roll(v, L - NEAR, 1) for v in (b0, b1, n))
    back = jnp.concatenate([jnp.where(low, rp, r0), jnp.where(low, r0, r1)], axis=1)
    ahead = jnp.concatenate([jnp.where(high, s1, s0), jnp.where(high, sn, s1)], axis=1)
    return back, ahead


def gathered(full, scale, k):
    rows = [
        jnp.concatenate([full[h, pl.ds(M * k + 16 * q, 16)].reshape(L, L) for q in (0, 1)], axis=1)
        for h in (0, 1)
    ]
    return split(jnp.concatenate(rows, axis=0) * scale)


def kernel(
    scale,
    x_in, cot_in, tf_in, tn_in, j_in,
    igv, grads, joins, full, th, tl, jth, jtl,
    xv, cotv, tfv, tnv, jv,
    xfar, xnear, dfar, dnear, dz,
    xh, xl, ah, al, ath, atl, dhl, zacc,
    sums, rc, ra1, rb1, s2a, s2b, ra2, rb2, ry,
    lsem, xs, xr, ds, dr, cs, cr,
    as1, ar1, bs1, br1, as2, ar2, bs2, br2, ys, yr,
    gas1, gar1, gbs1, gbr1, gas2, gar2, gbs2, gbr2, fas, far_, fbs, fbr,
):
    me = lax.axis_index("tm")
    c = lax.rem(me, 2)
    z = lax.rem(me // 2, Z)
    x = lax.rem(me // (2 * Z), X)
    y = me // (2 * Z * X)
    total = 2 * X * Y * Z

    def at(yy, xx, zz, cc):
        return ((yy * X + xx) * Z + zz) * 2 + cc

    def ypeer(d):
        return at(lax.rem(y + d, Y), x, z, c)

    def xpeer(d):
        return at(y, lax.rem(x + d, X), z, c)

    def zpeer(d):
        return at(y, x, lax.rem(z + d, Z), c)

    sibling = at(y, x, z, 1 - c)
    later, earlier = lax.rem(me + 1, total), lax.rem(me + total - 1, total)
    ys_, xs_, zs_ = range(1, Y), range(1, X), range(1, Z)
    zorder = [4, 3, 5, 2, 6, 1, 7]
    yorder = [4, 3, 5, 2, 6, 1, 7]
    xorder = [2, 1, 3]
    started = []

    def send(src, dst, ssem, rsem, device):
        copy = pltpu.make_async_remote_copy(
            src_ref=src, dst_ref=dst, send_sem=ssem, recv_sem=rsem, device_id=(device,), device_id_type=MESH
        )
        copy.start()
        started.append(copy)
        return copy

    def local(src, dst, sem):
        copy = pltpu.make_async_copy(src, dst, sem)
        copy.start()
        return copy

    partners = [ypeer(d) for d in ys_] + [xpeer(d) for d in xs_] + [zpeer(d) for d in zs_] + [later, earlier]
    barrier = pltpu.get_barrier_semaphore()
    for partner in partners + [at(y, x, z, 1 - c)]:
        pl.semaphore_signal(barrier, inc=1, device_id=(partner,), device_id_type=MESH)
    loads = [
        local(src, dst, lsem.at[k])
        for k, (src, dst) in enumerate(
            [(j_in, jv), (tf_in, tfv), (tn_in, tnv), (x_in, xv), (cot_in, cotv)]
        )
    ]
    pl.semaphore_wait(barrier, len(partners) + 1)

    up, down = ypeer(1), ypeer(Y - 1)
    xf = [
        send(x_in, xfar.at[0], xs.at[0], xr.at[0], up),
        send(x_in, xfar.at[1], xs.at[1], xr.at[1], down),
    ]
    xn = [
        send(x_in.at[:, pl.ds(L, L)], xnear.at[0], xs.at[2], xr.at[2], later),
        send(x_in.at[:, pl.ds(0, L)], xnear.at[1], xs.at[3], xr.at[3], earlier),
    ]
    one = lambda ok: jnp.where(ok, 1.0, 0.0).astype(F32)
    has_up, has_down = one(y < Y - 1), one(y > 0)
    has_later, has_earlier = one(me < total - 1), one(me > 0)

    def put(hi, lo, k, v):
        hi[k], lo[k] = split(v)

    def get(hi, lo, k):
        return hi[k], lo[k]

    for copy in loads[:3]:
        copy.wait()
    jf, jn = split(jv[:, :C]), split(jv[:, C:])
    for k in range(3):
        put(th, tl, k, tfv[k])
        put(th, tl, 3 + k, tnv[k])
    joined = [
        mm3(jf, get(th, tl, 0), NN),
        mm3(jf, get(th, tl, 2), NN),
        mm3(jn, get(th, tl, 3), NN),
        mm3(jn, get(th, tl, 5), NN),
        mm3(jf, get(th, tl, 1), NN) + mm3(jn, get(th, tl, 4), NN),
    ]
    for k, v in enumerate(joined):
        put(ah, al, k, v)
    for copy in loads[3:]:
        copy.wait()
    put(xh, xl, 4, xv[...])
    xn[0].wait_recv()
    xn[1].wait_recv()
    back, ahead = shifted(xv[:, :L], xv[:, L:], xnear[0] * has_earlier, xnear[1] * has_later)
    put(xh, xl, 2, back)
    put(xh, xl, 3, ahead)
    zacc[...] = sum(mm3(get(ah, al, k), get(xh, xl, k), NN) for k in (4, 2, 3))
    for k, v in enumerate(joined):
        put(ath, atl, k, v.T)
    put(jth, jtl, 0, jv[:, :C].T)
    put(jth, jtl, 1, jv[:, C:].T)

    xf[0].wait_recv()
    put(xh, xl, 0, xfar[0] * has_down)
    xf[1].wait_recv()
    put(xh, xl, 1, xfar[1] * has_up)
    zvalue = zacc[...] + (mm3(get(ah, al, 0), get(xh, xl, 0), NN) + mm3(get(ah, al, 1), get(xh, xl, 1), NN))
    dzvalue = cotv[...] * gelu_slope(zvalue)
    dz[...] = dzvalue
    dhl[pl.ds(0, C)], dhl[pl.ds(C, C)] = split(dzvalue)
    df = [
        send(dz, dfar.at[0], ds.at[0], dr.at[0], up),
        send(dz, dfar.at[1], ds.at[1], dr.at[1], down),
    ]

    order = [4] + [lax.rem(x + d, X) for d in xorder] + [x]
    core, p1a, p1b = [], [], []

    def multiply(i, k):
        hilo = lax.dot_general(dhl[...], xh[k], NT, preferred_element_type=F32)
        low = lax.dot_general(dhl[pl.ds(0, C)], xl[k], NT, preferred_element_type=F32)
        g = hilo[:C] + (hilo[C:] + low)
        for h in (0, 1):
            for q in (0, 1):
                sums[h, pl.ds(M * k + 16 * q, 16)] = g[L * h : L * h + L, L * q : L * q + L].reshape(16, 8, L)
        block = pl.ds(M * k, M)
        core.append(send(sums.at[1 - c, block], rc.at[block], cs.at[i], cr.at[i], sibling))

    def combine(i, k):
        core[i].wait_recv()
        block = pl.ds(M * k, M)
        sums[c, block] = sums[c, block] + rc[block]
        if i == 0:
            for d in zorder:
                part = sums.at[c, pl.ds(B0 + GB * lax.rem(z + d, Z), GB)]
                p1b.append(send(part, rb1.at[d - 1], bs1.at[d - 1], br1.at[d - 1], zpeer(d)))
        elif i <= 3:
            d = xorder[i - 1]
            p1a.append(send(sums.at[c, block], ra1.at[d - 1], as1.at[d - 1], ar1.at[d - 1], xpeer(d)))

    for i in (0, 1, 2):
        multiply(i, order[i])
    combine(0, order[0])
    multiply(3, order[3])
    combine(1, order[1])
    multiply(4, order[4])
    for i in (2, 3, 4):
        combine(i, order[i])

    def dsplit():
        return dhl[pl.ds(0, C)], dhl[pl.ds(C, C)]

    igv[...] = cotv[...] + mm3(get(ath, atl, 4), dsplit(), NN)
    for copy in p1a:
        copy.wait_recv()
    s2a[...] = sums[c, pl.ds(GA * x, GA)] + sum(ra1[d - 1] for d in xs_)
    p2a = [
        send(s2a.at[pl.ds(NA * lax.rem(z + d, Z), NA)], ra2.at[d - 1], as2.at[d - 1], ar2.at[d - 1], zpeer(d))
        for d in zorder
    ]
    for copy in p1b:
        copy.wait_recv()
    s2b[...] = sums[c, pl.ds(B0 + GB * z, GB)] + sum(rb1[d - 1] for d in zs_)
    p2b = [
        send(s2b.at[pl.ds(NB * lax.rem(x + d, X), NB)], rb2.at[d - 1], bs2.at[d - 1], br2.at[d - 1], xpeer(d))
        for d in xorder
    ]

    df[0].wait_recv()
    df[1].wait_recv()
    acc = mm3(get(ath, atl, 0), split(dfar[1] * has_up), NN) + mm3(get(ath, atl, 1), split(dfar[0] * has_down), NN)
    igv[...] = igv[...] + acc

    for copy in p2a + p2b:
        copy.wait_recv()
    mine = ry.at[y]
    mine[pl.ds(0, NA)] = s2a[pl.ds(NA * z, NA)] + sum(ra2[d - 1] for d in zs_)
    mine[pl.ds(NA, NB)] = s2b[pl.ds(NB * x, NB)] + sum(rb2[d - 1] for d in xs_)
    p3 = [send(mine, ry.at[y], ys.at[d - 1], yr.at[d - 1], ypeer(d)) for d in yorder]
    dn = [
        send(dz.at[:, pl.ds(L, L)], dnear.at[0], ds.at[2], dr.at[2], later),
        send(dz.at[:, pl.ds(0, L)], dnear.at[1], ds.at[3], dr.at[3], earlier),
    ]
    for copy in p3:
        copy.wait_recv()
    summed = ry[0]
    for k in range(1, Y):
        summed = summed + ry[k]
    fa = full.at[c, pl.ds(GA * x + NA * z, NA)]
    fb = full.at[c, pl.ds(B0 + GB * z + NB * x, NB)]
    fa[...] = summed[:NA]
    fb[...] = summed[NA:]

    g1a = {d: send(fa, fa, gas1.at[d - 1], gar1.at[d - 1], zpeer(d)) for d in zorder}
    g1b = [send(fb, fb, gbs1.at[d - 1], gbr1.at[d - 1], xpeer(d)) for d in xorder]

    def piece_a(d, j):
        return full.at[c, pl.ds(GA * lax.rem(x - d + X, X) + NA * lax.rem(z - j + Z, Z), NA)]

    def block_b(d):
        return full.at[c, pl.ds(B0 + GB * lax.rem(z - d + Z, Z), GB)]

    g2a, g2b, forward_a, forward_b = {}, {}, {}, {}

    def pass_a(d, j):
        piece = piece_a(d, j)
        forward_a[d, j] = send(piece, piece, fas.at[d, j], far_.at[d, j], sibling)
        if d == 0:
            for e in (1, 3, 2):
                g2a[e, j] = send(piece, piece, gas2.at[e - 1, j], gar2.at[e - 1, j], xpeer(e))

    def pass_b(d):
        block = block_b(d)
        forward_b[d] = send(block, block, fbs.at[d], fbr.at[d], sibling)
        if d == 0:
            for e in zorder:
                g2b[e] = send(block, block, gbs2.at[e - 1], gbr2.at[e - 1], zpeer(e))

    pass_a(0, 0)
    dn[0].wait_recv()
    dn[1].wait_recv()
    back, ahead = shifted(dz[:, :L], dz[:, L:], dnear[0] * has_earlier, dnear[1] * has_later)
    acc = mm3(get(ath, atl, 2), split(ahead), NN) + mm3(get(ath, atl, 3), split(back), NN)
    igv[...] = igv[...] + acc

    near_first = [1, 7, 2, 6, 3, 5, 4]
    for j in near_first[:2]:
        g1a[j].wait_recv()
        pass_a(0, j)
    for copy in g1b:
        copy.wait_recv()
    pass_b(0)
    for j in near_first[2:]:
        g1a[j].wait_recv()
        pass_a(0, j)

    def products(m):
        branch, tap = m // 2, 2 * lax.rem(m, 2)
        g = gathered(full, scale, m)
        grads[branch, tap] = mm3(get(jth, jtl, branch), g, NN)
        joins[branch] = joins[branch] + mm3(g, get(th, tl, 3 * branch + tap), NT)

    joins[...] = jnp.zeros_like(joins)
    for j in [0] + near_first:
        for d in (1, 3):
            g2a[d, j].wait_recv()
            pass_a(d, j)
        if j:
            g2b[j].wait_recv()
            pass_b(j)
    for j in [0] + near_first:
        g2a[2, j].wait_recv()
        pass_a(2, j)
    for d in (0, 1, 3, 2):
        for j in range(Z):
            forward_a[d, j].wait_recv()
        products(lax.rem(x - d + X, X))
    for copy in forward_b.values():
        copy.wait_recv()
    for copy in started:
        copy.wait_send()


def finish(scale, igv, grads, joins, full, th, tl, jth, jtl, ig_out, far_out, near_out, join_out, centre, joined, osem):
    copies = []

    def store(src, dst):
        copy = pltpu.make_async_copy(src, dst, osem.at[len(copies)])
        copy.start()
        copies.append(copy)

    store(igv, ig_out)
    outs = (far_out, near_out)
    for branch in (0, 1):
        for tap in (0, 2):
            store(grads.at[branch, tap], outs[branch].at[tap])
    g = gathered(full, scale, 4)
    for branch in (0, 1):
        joined[branch] = joins[branch] + mm3(g, (th[3 * branch + 1], tl[3 * branch + 1]), NT)
        store(joined.at[branch], join_out.at[:, pl.ds(C * branch, C)])
    for branch in (0, 1):
        centre[branch] = mm3((jth[branch], jtl[branch]), g, NN)
        store(centre.at[branch], outs[branch].at[1])
    for copy in copies:
        copy.wait()


def on_device(inputs, cotangent, taps_far, taps_near, joining):
    scale = 1.0 / math.sqrt(inputs.shape[1] * lax.axis_size("tm"))
    sq = (C, C)
    vm = lambda *shape: pltpu.VMEM(shape, F32)
    vb = lambda *shape: pltpu.VMEM(shape, BF16)
    dma = lambda *n: pltpu.SemaphoreType.DMA(n)
    anywhere = pl.BlockSpec(memory_space=pl.ANY)
    held = pl.BlockSpec(memory_space=pltpu.VMEM)
    scratch = (
        [vm(*sq), vm(*sq), vm(3, *sq), vm(3, *sq), vm(C, 2 * C)]
        + [vm(2, *sq), vm(2, C, L), vm(2, *sq), vm(2, C, L), vm(*sq)]
        + [vb(5, *sq)] * 4 + [vb(5, *sq)] * 2 + [vb(2 * C, C)]
        + [vm(*sq)]
        + [vm(2, 160, 8, L), vm(160, 8, L)]
        + [vm(X - 1, GA, 8, L), vm(Z - 1, GB, 8, L), vm(GA, 8, L), vm(GB, 8, L)]
        + [vm(Z - 1, NA, 8, L), vm(X - 1, NB, 8, L), vm(Y, NA + NB, 8, L)]
        + [dma(5), dma(4), dma(4), dma(4), dma(4), dma(5), dma(5)]
        + [dma(X - 1)] * 2 + [dma(Z - 1)] * 2 + [dma(Z - 1)] * 2 + [dma(X - 1)] * 2 + [dma(Y - 1)] * 2
        + [dma(Z - 1)] * 2 + [dma(X - 1)] * 2 + [dma(X - 1, Z)] * 2 + [dma(Z - 1)] * 2
        + [dma(X, Z)] * 2 + [dma(Z)] * 2
    )
    args = [pltpu.with_memory_space_constraint(v, pltpu.HBM) for v in (inputs, cotangent, taps_far, taps_near, joining)]
    shape = jax.ShapeDtypeStruct
    passed = pl.pallas_call(
        functools.partial(kernel, scale),
        out_shape=[
            shape(sq, F32), shape((2, 3, *sq), F32), shape((2, *sq), F32), shape((2, 160, 8, L), F32), shape((6, *sq), BF16), shape((6, *sq), BF16),
            shape((2, *sq), BF16), shape((2, *sq), BF16),
        ],
        in_specs=[anywhere] * 5,
        out_specs=[held] * 8,
        scratch_shapes=scratch,
        compiler_params=pltpu.CompilerParams(
            collective_id=0, has_side_effects=True, vmem_limit_bytes=32 * 1024 * 1024
        ),
    )(*args)
    return pl.pallas_call(
        functools.partial(finish, scale),
        out_shape=[shape(sq, F32), shape((3, *sq), F32), shape((3, *sq), F32), shape((C, 2 * C), F32)],
        in_specs=[held] * 8,
        out_specs=[anywhere] * 4,
        scratch_shapes=[vm(2, *sq), vm(2, *sq), dma(9)],
        compiler_params=pltpu.CompilerParams(vmem_limit_bytes=32 * 1024 * 1024),
    )(*passed)


def solution(mesh):
    in_specs = (P(None, "tm"), P(None, "tm"), P(), P(), P())
    out_specs = (P(None, "tm"), P(), P(), P())
    return jax.shard_map(
        on_device, mesh=mesh, in_specs=in_specs, out_specs=out_specs, check_vma=False
    )
```

time: 71 us -> 63.3 us (0.89)
  local copies, waits for them, and re-layouts: 8.45 us -> 0 us
  Pallas kernels: 61.5 us -> 62.3 us
    unnamed x14 -> x0, local copies, waits for them, and re-layouts: 8.45 us -> none
    pallas_call x1 -> x2, Pallas kernels: 61.5 us -> 62.3 us  [the longest x1 60.8 us: on_device(): pl.pallas_call(functools.partial(kernel, scale), out_shape=[shape(sq, F32...]
where the time goes in v2:
time: 63.3 us; the launch traced here: 63 us
  Pallas kernels  62.3 us (98%)
  between operations  0.64 us (1%)
    pallas_call x1, Pallas kernels, on_device(): pl.pallas_call(functools.partial(kernel, scale), out_shape=[shape(sq, F32...  60.8 us
    pallas_call x1, Pallas kernels, on_device(): pl.pallas_call(functools.partial(finish, scale), out_shape=[shape(sq, F32...  1.5 us

profile of v2, /device:TPU:1, one launch (start us, length us, event | category | flops | bytes accessed | tf_op | source)
XLA Modules:
  0.0 63.0 jit_solution(484274251292381468)
XLA Ops:
  0.6 60.8 %shard_map.84 = (f32[256,256]{1,0:T(8,128)S(1)}, f32[2,3,256,256]{3,2,1,0:T(8,128)S(1)}, f32[2,256,256]{2,1,0:T(8,128)S(1)}, f32[2,160,8,128]{3,2,1,0:T(8,128)S(...) custom-call(f32[256,256]{1,0:T(8,128)} %x_in.1, ...), custom_call_target="tpu_custom_call" | custom-call | tf_op jit(solution)/shard_map/pallas_call | solution.py:384
  61.5 1.5 %shard_map.85 = (f32[256,256]{1,0:T(8,128)}, f32[3,256,256]{2,1,0:T(8,128)}, f32[3,256,256]{2,1,0:T(8,128)}, f32[256,512]{1,0:T(8,128)}) custom-call(f32[256,256]{1,0:T(8,128)S(1)} %get-tuple-element.12.igv, f32[2,3,256,256]{3,2,1,0:T(8,128)S(1)} %get-tuple-element.13.grads, f32[2,256,256]{2,1,0:T(8,128)S(1)} %get-tuple-element.14.joins, ...), custom_call_target="tpu_custom_call" | custom-call | tf_op jit(solution)/shard_map/pallas_call | solution.py:397

commit v3 on v2

--- a/solution.py
+++ b/solution.py
@@ -187,7 +187,8 @@
     ]
 
     order = [4] + [lax.rem(x + d, X) for d in xorder] + [x]
-    core, p1a, p1b = [], [], []
+    core, p1a, p1b, p2a = [], {}, [], []
+    far_first = zorder + [0]
 
     def multiply(i, k):
         hilo = lax.dot_general(dhl[...], xh[k], NT, preferred_element_type=F32)
@@ -209,7 +210,10 @@
                 p1b.append(send(part, rb1.at[d - 1], bs1.at[d - 1], br1.at[d - 1], zpeer(d)))
         elif i <= 3:
             d = xorder[i - 1]
-            p1a.append(send(sums.at[c, block], ra1.at[d - 1], as1.at[d - 1], ar1.at[d - 1], xpeer(d)))
+            for j in far_first:
+                zz = NA * lax.rem(z + j, Z)
+                part = sums.at[c, pl.ds(M * k + zz, NA)]
+                p1a[d, j] = send(part, ra1.at[d - 1, pl.ds(zz, NA)], as1.at[d - 1, j], ar1.at[d - 1, j], xpeer(d))
 
     for i in (0, 1, 2):
         multiply(i, order[i])
@@ -223,14 +227,14 @@
     def dsplit():
         return dhl[pl.ds(0, C)], dhl[pl.ds(C, C)]
 
-    igv[...] = cotv[...] + mm3(get(ath, atl, 4), dsplit(), NN)
-    for copy in p1a:
-        copy.wait_recv()
-    s2a[...] = sums[c, pl.ds(GA * x, GA)] + sum(ra1[d - 1] for d in xs_)
-    p2a = [
-        send(s2a.at[pl.ds(NA * lax.rem(z + d, Z), NA)], ra2.at[d - 1], as2.at[d - 1], ar2.at[d - 1], zpeer(d))
-        for d in zorder
-    ]
+    for j in far_first:
+        for d in xorder:
+            p1a[d, j].wait_recv()
+        zz = NA * lax.rem(z + j, Z)
+        piece = pl.ds(zz, NA)
+        s2a[piece] = sums[c, pl.ds(GA * x + zz, NA)] + sum(ra1[d - 1, piece] for d in xs_)
+        if j:
+            p2a.append(send(s2a.at[piece], ra2.at[j - 1], as2.at[j - 1], ar2.at[j - 1], zpeer(j)))
     for copy in p1b:
         copy.wait_recv()
     s2b[...] = sums[c, pl.ds(B0 + GB * z, GB)] + sum(rb1[d - 1] for d in zs_)
@@ -239,6 +243,7 @@
         for d in xorder
     ]
 
+    igv[...] = cotv[...] + mm3(get(ath, atl, 4), dsplit(), NN)
     df[0].wait_recv()
     df[1].wait_recv()
     acc = mm3(get(ath, atl, 0), split(dfar[1] * has_up), NN) + mm3(get(ath, atl, 1), split(dfar[0] * has_down), NN)
@@ -375,7 +380,7 @@
         + [vm(X - 1, GA, 8, L), vm(Z - 1, GB, 8, L), vm(GA, 8, L), vm(GB, 8, L)]
         + [vm(Z - 1, NA, 8, L), vm(X - 1, NB, 8, L), vm(Y, NA + NB, 8, L)]
         + [dma(5), dma(4), dma(4), dma(4), dma(4), dma(5), dma(5)]
-        + [dma(X - 1)] * 2 + [dma(Z - 1)] * 2 + [dma(Z - 1)] * 2 + [dma(X - 1)] * 2 + [dma(Y - 1)] * 2
+        + [dma(X - 1, Z)] * 2 + [dma(Z - 1)] * 2 + [dma(Z - 1)] * 2 + [dma(X - 1)] * 2 + [dma(Y - 1)] * 2
         + [dma(Z - 1)] * 2 + [dma(X - 1)] * 2 + [dma(X - 1, Z)] * 2 + [dma(Z - 1)] * 2
         + [dma(X, Z)] * 2 + [dma(Z)] * 2
     )

time: 63.3 us -> 63.6 us (level)
  no operation moved by 1% of the time
where the time goes in v3:
time: 63.6 us; the launch traced here: 63.4 us
  Pallas kernels  62.8 us (99%)
  between operations  0.64 us (1%)
    pallas_call x1, Pallas kernels, on_device(): pl.pallas_call(functools.partial(kernel, scale), out_shape=[shape(sq, F32...  61.3 us
    pallas_call x1, Pallas kernels, on_device(): pl.pallas_call(functools.partial(finish, scale), out_shape=[shape(sq, F32...  1.5 us

profile of v3, /device:TPU:1, one launch (start us, length us, event | category | flops | bytes accessed | tf_op | source)
XLA Modules:
  0.0 63.4 jit_solution(8991463235954442817)
XLA Ops:
  0.6 61.3 %shard_map.84 = (f32[256,256]{1,0:T(8,128)S(1)}, f32[2,3,256,256]{3,2,1,0:T(8,128)S(1)}, f32[2,256,256]{2,1,0:T(8,128)S(1)}, f32[2,160,8,128]{3,2,1,0:T(8,128)S(...) custom-call(f32[256,256]{1,0:T(8,128)} %x_in.1, ...), custom_call_target="tpu_custom_call" | custom-call | tf_op jit(solution)/shard_map/pallas_call | solution.py:389
  61.9 1.5 %shard_map.85 = (f32[256,256]{1,0:T(8,128)}, f32[3,256,256]{2,1,0:T(8,128)}, f32[3,256,256]{2,1,0:T(8,128)}, f32[256,512]{1,0:T(8,128)}) custom-call(f32[256,256]{1,0:T(8,128)S(1)} %get-tuple-element.12.igv, f32[2,3,256,256]{3,2,1,0:T(8,128)S(1)} %get-tuple-element.13.grads, f32[2,256,256]{2,1,0:T(8,128)S(1)} %get-tuple-element.14.joins, ...), custom_call_target="tpu_custom_call" | custom-call | tf_op jit(solution)/shard_map/pallas_call | solution.py:402
